TPU v7x, 32 devices: a whole 2x2x4 slice. The times are simulated.
32 devices in a mesh: dp: 8 (over z, y), mp: 4 (over x, core).
Axes of the slice: x: 2, y: 2, z: 4, core: 2. Of those that a mesh axis runs over, the one named last changes fastest.
Arguments:
- pre_act: bfloat16 [1024, 36864], P('dp', 'mp'), may hold values from -6 to 6
- grad_out: bfloat16 [1024, 18432], P('dp', 'mp'), may hold values from -6 to 6
- row_state: float32 [4, 4608], P(None, 'dp'), may hold values from 3e-05 to 0.0003
- col_state: float32 [36864], P('mp'), may hold values from 3e-05 to 0.0003
Outputs:
- update: bfloat16 [4, 4608, 36864], P(None, 'dp', 'mp')
- row_new: float32 [4, 4608], P(None, 'dp')
- col_new: float32 [36864], P('mp')
All inputs are finite; a program needn't handle non-finite values.
Results may differ from a plain program's by a relative error of at most 0.0015.
The roundings to bfloat16 on the way count: a program that leaves them out, or rounds other values in their place, can miss the bound.
Values may be sent and summed in bfloat16 or wider, within the bound.
A program may use at most 192 MiB of HBM per device.

v0:
```python
import jax
import jax.numpy as jnp
from jax import lax
from jax.sharding import PartitionSpec as P

D = 18432


decay = 1.0 - 2.0 ** (-0.8)
tiny = 1e-30


def body(pre_act, grad_out, row_state, col_state):
    dp_count = lax.axis_size("dp")
    mp_count = lax.axis_size("mp")
    tok_rows = pre_act.shape[0]
    hid_cols = pre_act.shape[1]
    all_tokens = tok_rows * dp_count
    all_hidden = hid_cols * mp_count
    slice_width = row_state.shape[1]
    own_width = mp_count * slice_width
    hidden = jax.nn.gelu(pre_act.astype(jnp.float32)).astype(jnp.bfloat16)
    full_out = lax.all_gather(grad_out, "mp", axis=1, tiled=True)
    split_out = full_out.reshape(tok_rows, mp_count, dp_count, slice_width)
    moved = lax.all_to_all(split_out, "dp", split_axis=2, concat_axis=0, tiled=True)
    own_cols = moved.reshape(all_tokens, own_width)
    product = lax.dot_general(
        own_cols,
        lax.all_gather(hidden, "dp", axis=0, tiled=True),
        (((0,), (0,)), ((), ())),
        preferred_element_type=jnp.float32,
    )
    grad = product / all_tokens
    squares = grad * grad
    row_flat = row_state.reshape(own_width)
    row_sum = lax.psum(jnp.sum(squares, axis=1), "mp")
    col_sum = lax.psum(jnp.sum(squares, axis=0), "dp")
    row_new = decay * row_flat + (1.0 - decay) * (row_sum / all_hidden + tiny)
    col_new = decay * col_state + (1.0 - decay) * (col_sum / D + tiny)
    scale = lax.psum(jnp.sum(row_new), "dp") / D
    update = (grad * lax.rsqrt(row_new[:, None] * col_new[None, :] / scale)).astype(jnp.bfloat16)
    return (
        update.reshape(mp_count, slice_width, hid_cols),
        row_new.reshape(mp_count, slice_width),
        col_new,
    )


def solution(mesh):
    return jax.shard_map(
        body,
        mesh=mesh,
        in_specs=(P("dp", "mp"), P("dp", "mp"), P(None, "dp"), P("mp")),
        out_specs=(P(None, "dp", "mp"), P(None, "dp"), P("mp")),
        check_vma=False,
    )
```

profile of v0, /device:TPU:0, one launch (start us, length us, event | category | flops | bytes accessed | tf_op | source)
XLA Modules:
  0.0 622.0 jit_solution(10696252309068730148)
XLA Ops:
  7.2 0.0 copy-start
  7.2 0.0 all-gather.5.cloned.1.call-start
  7.2 2.5 copy.9
  9.7 0.0 all-gather.5.cloned.1.call-update
  9.8 0.0 all-gather.3.cloned.1.call-start
  9.8 0.0 copy-done
  9.8 3.0 fusion.8
  12.9 0.0 all-gather.3.cloned.1.call-update
  12.9 37.4 %all-gather.5.cloned.1.call-done = bf16[128,18432]{0,1:T(8,128)(2,1)} async-done(((bf16[128,4608]{0,1:T(8,128)(2,1)}), bf16[128,18432]{0,1:T(8,128)(2,1)}) %all-gather.5.cloned.1.call-update) | async-done | bytes 4718608 | tf_op jit(solution)/shard_map/all_gather | solution.py:23
  50.3 4.9 copy.10
  55.2 0.0 copy-start.3
  55.2 5.6 all-to-all-start
  60.9 0.0 copy-done.3
  60.9 0.1 mul.76
  61.0 156.0 %all-to-all-done = bf16[128,4,8,576]{0,3,1,2:T(8,128)(2,1)} async-done(((bf16[128,4,8,576]{0,3,1,2:T(8,128)(2,1)}), bf16[128,4,8,576]{0,3,1,2:T(8,128)(2,1)}, u32[]{:S(2)}, u32[]{:S(2)}) %all-to-all-start) | async-done | bytes 4718624 | tf_op jit(solution)/shard_map/all_to_all | solution.py:25
  217.0 7.6 %copy.11 = bf16[8,128,4,1,576]{1,0,4,2,3:T(8,128)(2,1)} copy(bf16[8,128,4,1,576]{1,4,2,0,3:T(8,128)(2,1)} %bitcast.2) | data formatting | bytes 9437184 | tf_op jit(solution)/shard_map/all_to_all | solution.py:25
  224.6 240.3 %all-gather.3.cloned.1.call-done = bf16[1024,9216]{1,0:T(8,128)(2,1)} async-done(((bf16[128,9216]{1,0:T(8,128)(2,1)}), bf16[1024,9216]{1,0:T(8,128)(2,1)}) %all-gather.3.cloned.1.call-update) | async-done | bytes 18874384 | tf_op jit(solution)/shard_map/all_gather | solution.py:29
  464.9 0.0 copy-start.2
  464.9 58.0 %fusion.1 = (f32[9216]{0:T(1024)S(1)}, f32[2304]{0:T(1024)S(1)}, f32[9216,2304]{0,1:T(8,128)}) fusion(bf16[1024,9216]{1,0:T(8,128)(2,1)} %all-gather.3.cloned.1.call-done, bf16[288,8,8,128]{3,2,1,0:T(8,128)(2,1)} %bitcast.26), kind=kOutput, calls=%fused_computation.3 | convolution fusion | flops 43571466240 | bytes 108573696 | tf_op jit(solution)/shard_map/dot_general | solution.py:27
  522.9 11.1 %psum.21 = f32[2304]{0:T(1024)S(1)} all-reduce(f32[2304]{0:T(1024)S(1)} %get-tuple-element.4), channel_id=1, replica_groups=mesh['dp'=8,'mp'=4] {'mp'}, use_global_device_ids=true, to_apply=%region_1.0 | all-reduce | flops 2304 | bytes 18432 | tf_op jit(solution)/shard_map/psum | solution.py:36
  534.0 0.6 fusion.12
  534.6 0.7 reshape.27
  535.3 37.6 %all-reduce = (f32[]{:T(128)}, f32[9216]{0:T(1024)S(1)}) all-reduce(f32[]{:T(128)} %get-tuple-element.7, f32[9216]{0:T(1024)S(1)} %get-tuple-element.3), channel_id=1, replica_groups=mesh['dp'=8,'mp'=4] {'dp'}, use_global_device_ids=true, to_apply=%region_5.0 | all-reduce | flops 9217 | bytes 73736 | tf_op jit(solution)/shard_map/psum | solution.py:40
  573.6 0.0 copy-done.2
  573.6 0.0 copy-start.1
  573.6 41.5 %fusion = bf16[2304,9216]{1,0:T(8,128)(2,1)} fusion(f32[9216,2304]{0,1:T(8,128)} %get-tuple-element.9, f32[]{:T(128)S(6)} %div.36, f32[9216]{0:T(1024)S(1)} %multiply_add_fusion, f32[2304]{0:T(1024)S(1)} %get-tuple-element.8), kind=kLoop, calls=%fused_computation.2 | loop fusion | flops 106168320 | bytes 127448064 | tf_op jit(solution)/shard_map/convert_element_type | solution.py:41
  615.2 0.0 copy-done.1
  (2 shorter events, 0.0 us)
Async XLA Ops:
  7.2 2.7 copy-start
  7.2 43.2 %all-gather.5.cloned.1.call-start = ((), (), s32[]{:S(2)}) async-start(), calls=%async_computation.2 | async-start | bytes 5898240 | tf_op jit(solution)/shard_map/all_gather | solution.py:23
  9.8 455.2 %all-gather.3.cloned.1.call-start = ((), (), s32[]{:S(2)}) async-start(), calls=%async_computation.1 | async-start | bytes 21233664 | tf_op jit(solution)/shard_map/all_gather | solution.py:29
  55.2 5.7 copy-start.3
  55.2 161.8 %all-to-all-start = ((bf16[128,4,8,576]{0,3,1,2:T(8,128)(2,1)}), bf16[128,4,8,576]{0,3,1,2:T(8,128)(2,1)}, u32[]{:S(2)}, u32[]{:S(2)}) async-start(bf16[128,4,8,576]{0,3,1,2:T(8,128)(2,1)} %copy.10), calls=%async_computation | async-start | bytes 9437184 | tf_op jit(solution)/shard_map/all_to_all | solution.py:25
  464.9 108.7 %copy-start.2 = (f32[9216]{0:T(1024)S(1)}, f32[9216]{0:T(1024)}, u32[]{:S(2)}) copy-start(f32[9216]{0:T(1024)} %param.7) | copy-start | bytes 110596
  573.6 41.6 %copy-start.1 = (f32[9216]{0:T(1024)}, f32[9216]{0:T(1024)S(1)}, u32[]{:S(2)}) copy-start(f32[9216]{0:T(1024)S(1)} %multiply_add_fusion) | copy-start | bytes 110596
Sparse Core Ops, SparseCore 0:
  10.1 40.1 all-gather.4
  51.9 413.0 all-gather.2
where the time goes:
time: 622 us
  waiting for transfers between devices  434 us (70%)
  matrix products  58 us (9%)
  blocking collectives  48.7 us (8%)
  other arithmetic  45.2 us (7%)
  local copies, waits for them, and re-layouts  15.8 us (3%)
  between operations  14.7 us (2%)
    all_gather x1, waiting for transfers between devices, body(): lax.all_gather(hidden, 'dp', axis=0, tiled=True)  240 us
    all_to_all x1, waiting for transfers between devices, body(): lax.all_to_all(split_out, 'dp', split_axis=2, concat_axis=0, tiled=True)  156 us
    dot_general x1, matrix products, body(): lax.dot_general(own_cols, lax.all_gather(hidden, 'dp', axis=0, tiled=True...  58 us
    convert_element_type x1, other arithmetic, body(): (grad * lax.rsqrt(row_new[:, None] * col_new[None, :] / scale)).astype(jn...  41.5 us
    psum x1, blocking collectives, body(): scale = lax.psum(jnp.sum(row_new), 'dp') / D  37.6 us
    all_gather x1, waiting for transfers between devices, body(): full_out = lax.all_gather(grad_out, 'mp', axis=1, tiled=True)  37.4 us
  transfers between devices with their start and end apart: 3, of which 3 were waited for; matrix products, arithmetic and copies ran while one was open for 3% of the time, Pallas kernels for 0%

commit v1 on v0

v1 whole, which is shorter than its diff:
```python
import functools

import jax
import jax.numpy as jnp
from jax import lax
from jax.experimental import pallas as pl
from jax.experimental.pallas import tpu as pltpu
from jax.sharding import PartitionSpec as P

D = 18432
MESH = pl.DeviceIdType.MESH
VMEM = pltpu.VMEM

decay = 1.0 - 2.0 ** (-0.8)
tiny = 1e-30

PIECES = 18
G_SEND_STEP = 2
G_READY_STEP = 8


def gather_kernel(
    dp_count, mp_count, pieces,
    pre_ref, g_ref, row_ref, col_ref,
    hid_out, gt_out, row_new, col_new, scale_out,
    hid, gt, row_acc, row_part, col_part, total_part,
    up_sem, down_sem, side_sem, recv_sem,
    g_local, g_send, g_recv, m_send, m_recv,
    out_sem, gt_sem, r_send, r_recv, c_send, c_recv, t_send, t_recv,
):
    rows = pre_ref.shape[0]
    width = hid.shape[2]
    depth = dp_count // 2
    slice_width = gt.shape[1]
    tokens = rows * dp_count
    d = lax.axis_index("dp")
    a = lax.axis_index("mp")
    z = d // 2
    y = d % 2
    period = 2 * max(depth - 1, 1)

    def peer(i):
        return lax.rem(d + i, dp_count)

    def mate(j):
        return lax.rem(a + j, mp_count)

    barrier = pltpu.get_barrier_semaphore()
    for i in range(1, dp_count):
        pl.semaphore_signal(barrier, inc=1, device_id=(peer(i), a), device_id_type=MESH)
    for j in range(1, mp_count):
        pl.semaphore_signal(barrier, inc=1, device_id=(d, mate(j)), device_id_type=MESH)
    pl.semaphore_wait(barrier, dp_count + mp_count - 2)

    def remote(src, dst, send, recv, device):
        return pltpu.make_async_remote_copy(
            src_ref=src, dst_ref=dst, send_sem=send, recv_sem=recv,
            device_id=device, device_id_type=MESH,
        )

    def tok(dev):
        return pl.ds(pl.multiple_of(dev * rows, rows), rows)

    own_g = pltpu.make_async_copy(g_ref.at[d], gt.at[a, :, tok(d)], g_local)
    own_g.start()
    for i in range(1, dp_count):
        remote(g_ref.at[peer(i)], gt.at[a, :, tok(d)], g_send.at[i], g_recv.at[i], (peer(i), a)).start()

    def spread_g():
        own_g.wait()
        for i in range(1, dp_count):
            src = lax.rem(d - i + dp_count, dp_count)
            block = gt.at[a, :, tok(src)]
            remote(block, block, g_send.at[i], g_recv.at[i], (peer(i), a)).wait_recv()
        for j in range(1, mp_count):
            remote(gt.at[a], gt.at[a], m_send.at[j], m_recv.at[j], (d, mate(j))).start()

    def finish_g():
        for j in range(1, mp_count):
            src = lax.rem(a - j + mp_count, mp_count)
            remote(gt.at[src], gt.at[src], m_send.at[j], m_recv.at[j], (d, mate(j))).wait_recv()
        pltpu.make_async_copy(gt, gt_out, gt_sem).start()

    def block_of(src, p):
        return hid.at[p, tok(src)]

    def arrive(src, p):
        block = block_of(src, p)
        remote(block, block, side_sem.at[src, p], recv_sem.at[src, p], (d, a)).wait_recv()

    def side_first(p):
        return lax.rem(p, period) == min(2, period - 1)

    def push(go, src, p, up, down, side):
        block = block_of(src, p)
        for wanted, sem, dev in ((up, up_sem, d + 2), (down, down_sem, d - 2), (side, side_sem, z * 2 + 1 - y)):
            if wanted is None:
                continue

            @pl.when(wanted)
            def _(sem=sem, dev=dev):
                copy = remote(block, block, sem.at[src, p], recv_sem.at[src, p], (dev, a))
                if go:
                    copy.start()
                else:
                    copy.wait_send()

    up_ok = z + 1 < depth
    down_ok = z > 0
    always = z >= 0

    def events(t, go):
        @pl.when(t < pieces)
        def _():
            if go:
                cols = pl.ds(pl.multiple_of(t * width, width), width)
                part = jax.nn.gelu(pre_ref[:, cols].astype(jnp.float32)).astype(jnp.bfloat16)
                hid[t, tok(d), :] = part
            push(go, d, t, up_ok, down_ok, always)

        def passing(zs, ys, p, valid, up, down, side):
            @pl.when(valid)
            def _():
                src = zs * 2 + ys
                if go:
                    arrive(src, p)
                push(go, src, p, up, down, side)

        for k in range(1, depth):
            p = t - k
            live = (p >= 0) & (p < pieces)
            row_first = jnp.logical_not(side_first(p))
            passing(z - k, y, p, live & (z - k >= 0), up_ok, None, row_first)
            passing(z + k, y, p, live & (z + k < depth), None, down_ok, row_first)
        for k in range(depth):
            p = t - k - 1
            live = (p >= 0) & (p < pieces) & side_first(p)
            if k == 0:
                passing(z, 1 - y, p, live, up_ok, down_ok, None)
            else:
                passing(z - k, 1 - y, p, live & (z - k >= 0), up_ok, None, None)
                passing(z + k, 1 - y, p, live & (z + k < depth), None, down_ok, None)

    row_acc[...] = jnp.zeros_like(row_acc)

    def work(c):
        @pl.when(jnp.logical_not(side_first(c)))
        def _():
            for zs in range(depth):
                arrive(zs * 2 + 1 - y, c)

        pltpu.make_async_copy(hid.at[c], hid_out.at[c], out_sem.at[c]).start()
        block = hid[c]

        def one(m, col):
            prod = jnp.dot(gt[m], block, preferred_element_type=jnp.float32)
            sq = prod * prod
            part = sq[:, 0:128]
            for q in range(1, width // 128):
                part = part + sq[:, q * 128:(q + 1) * 128]
            row_acc[m] += part
            return col + jnp.sum(sq, axis=0, keepdims=True)

        col = lax.fori_loop(0, mp_count, one, jnp.zeros((1, width), jnp.float32))
        col_part[d, pl.ds(c, 1), :] = col

    def done_by(t):
        return jnp.clip(jnp.minimum(2 * (t - G_READY_STEP + 1), t - depth + 1), 0, pieces)

    steps = pieces + depth

    @pl.loop(0, steps)
    def _(t):
        events(t, True)

        @pl.when(t == G_SEND_STEP)
        def _():
            spread_g()

        @pl.when(t == G_READY_STEP)
        def _():
            finish_g()

        @pl.loop(done_by(t - 1), done_by(t))
        def _(c):
            work(c)

    ones = jnp.ones((8, 128), jnp.float32)
    for m in range(mp_count):
        turned = lax.dot_general(
            ones, row_acc[m], (((1,), (1,)), ((), ())),
            precision=lax.Precision.HIGHEST, preferred_element_type=jnp.float32,
        )
        row_part[a, m:m + 1, :] = turned[0:1]
    for j in range(1, mp_count):
        remote(row_part.at[a], row_part.at[a], r_send.at[j], r_recv.at[j], (d, mate(j))).start()
    for i in range(1, dp_count):
        remote(col_part.at[d], col_part.at[d], c_send.at[i], c_recv.at[i], (peer(i), a)).start()

    for j in range(1, mp_count):
        src = lax.rem(a - j + mp_count, mp_count)
        remote(row_part.at[src], row_part.at[src], r_send.at[j], r_recv.at[j], (d, mate(j))).wait_recv()
    inv = 1.0 / (tokens * tokens)
    all_hidden = pieces * width * mp_count
    row_sum = row_part[0]
    for m in range(1, mp_count):
        row_sum = row_sum + row_part[m]
    new = decay * row_ref[...] + (1.0 - decay) * (row_sum * inv / all_hidden + tiny)
    row_new[...] = new
    own_total = jnp.sum(jnp.sum(new, axis=1, keepdims=True), axis=0, keepdims=True)
    total_part[d] = jnp.broadcast_to(own_total, (8, 128))
    for i in range(1, dp_count):
        remote(total_part.at[d], total_part.at[d], t_send.at[i], t_recv.at[i], (peer(i), a)).start()

    for i in range(1, dp_count):
        src = lax.rem(d - i + dp_count, dp_count)
        remote(col_part.at[src], col_part.at[src], c_send.at[i], c_recv.at[i], (peer(i), a)).wait_recv()
    col_sum = col_part[0]
    for i in range(1, dp_count):
        col_sum = col_sum + col_part[i]
    col_new[...] = decay * col_ref[...] + (1.0 - decay) * (col_sum * inv / D + tiny)

    for i in range(1, dp_count):
        src = lax.rem(d - i + dp_count, dp_count)
        remote(total_part.at[src], total_part.at[src], t_send.at[i], t_recv.at[i], (peer(i), a)).wait_recv()
    total = total_part[0]
    for i in range(1, dp_count):
        total = total + total_part[i]
    scale_out[...] = total / D

    @pl.loop(0, steps)
    def _(t):
        events(t, False)

    for i in range(1, dp_count):
        remote(g_ref.at[peer(i)], gt.at[a, :, tok(d)], g_send.at[i], g_recv.at[i], (peer(i), a)).wait_send()
        remote(col_part.at[d], col_part.at[d], c_send.at[i], c_recv.at[i], (peer(i), a)).wait_send()
        remote(total_part.at[d], total_part.at[d], t_send.at[i], t_recv.at[i], (peer(i), a)).wait_send()
    for j in range(1, mp_count):
        remote(gt.at[a], gt.at[a], m_send.at[j], m_recv.at[j], (d, mate(j))).wait_send()
        remote(row_part.at[a], row_part.at[a], r_send.at[j], r_recv.at[j], (d, mate(j))).wait_send()
    pltpu.make_async_copy(gt, gt_out, gt_sem).wait()

    @pl.loop(0, pieces)
    def _(c):
        pltpu.make_async_copy(hid.at[c], hid_out.at[c], out_sem.at[c]).wait()


def update_kernel(gt_ref, hid_ref, row_ref, col_ref, out_ref):
    block = hid_ref[0]
    col = col_ref[0]

    @pl.loop(0, gt_ref.shape[0])
    def _(m):
        prod = jnp.dot(gt_ref[m], block, preferred_element_type=jnp.float32)
        out_ref[m] = (prod * row_ref[m] * col).astype(jnp.bfloat16)


def body(pre_act, grad_out, row_state, col_state):
    dp_count = lax.axis_size("dp")
    mp_count = lax.axis_size("mp")
    rows, hid_cols = pre_act.shape
    tokens = rows * dp_count
    slice_width = row_state.shape[1]
    pieces = PIECES
    width = hid_cols // pieces
    f32, bf16 = jnp.float32, jnp.bfloat16
    g_blocks = grad_out.reshape(rows, dp_count, slice_width).transpose(1, 2, 0)
    whole = pl.BlockSpec(memory_space=VMEM)
    anywhere = pl.BlockSpec(memory_space=pl.ANY)
    dma = pltpu.SemaphoreType.DMA
    flops = 2 * tokens * mp_count * slice_width * hid_cols
    hid, gt, row_new, col_new, scale = pl.pallas_call(
        functools.partial(gather_kernel, dp_count, mp_count, pieces),
        out_shape=(
            jax.ShapeDtypeStruct((pieces, tokens, width), bf16),
            jax.ShapeDtypeStruct((mp_count, slice_width, tokens), bf16),
            jax.ShapeDtypeStruct((mp_count, slice_width), f32),
            jax.ShapeDtypeStruct((pieces, width), f32),
            jax.ShapeDtypeStruct((8, 128), f32),
        ),
        in_specs=[whole] * 4,
        out_specs=(anywhere, anywhere, whole, whole, whole),
        scratch_shapes=[
            VMEM((pieces, tokens, width), bf16),
            VMEM((mp_count, slice_width, tokens), bf16),
            VMEM((mp_count, slice_width, 128), f32),
            VMEM((mp_count, mp_count, slice_width), f32),
            VMEM((dp_count, pieces, width), f32),
            VMEM((dp_count, 8, 128), f32),
            dma((dp_count, pieces)), dma((dp_count, pieces)), dma((dp_count, pieces)), dma((dp_count, pieces)),
            dma, dma((dp_count,)), dma((dp_count,)), dma((mp_count,)), dma((mp_count,)),
            dma((pieces,)), dma, dma((mp_count,)), dma((mp_count,)),
            dma((dp_count,)), dma((dp_count,)), dma((dp_count,)), dma((dp_count,)),
        ],
        compiler_params=pltpu.CompilerParams(
            collective_id=0, has_side_effects=True, vmem_limit_bytes=56 * 2**20
        ),
        cost_estimate=pl.CostEstimate(
            flops=flops, bytes_accessed=2 * tokens * hid_cols * 2, transcendentals=rows * hid_cols
        ),
    )(pre_act, g_blocks, row_state, col_state.reshape(pieces, width))
    row_factor = lax.rsqrt(row_new / scale[0, 0]) / tokens
    col_factor = lax.rsqrt(col_new)
    update = pl.pallas_call(
        update_kernel,
        grid=(pieces,),
        out_shape=jax.ShapeDtypeStruct((mp_count, slice_width, hid_cols), bf16),
        in_specs=[
            pl.BlockSpec((mp_count, slice_width, tokens), lambda i: (0, 0, 0)),
            pl.BlockSpec((1, tokens, width), lambda i: (i, 0, 0)),
            pl.BlockSpec((mp_count, slice_width, 1), lambda i: (0, 0, 0)),
            pl.BlockSpec((1, 1, width), lambda i: (i, 0, 0)),
        ],
        out_specs=pl.BlockSpec((mp_count, slice_width, width), lambda i: (0, 0, i)),
        compiler_params=pltpu.CompilerParams(vmem_limit_bytes=56 * 2**20),
        cost_estimate=pl.CostEstimate(
            flops=flops, bytes_accessed=2 * (tokens + mp_count * slice_width) * hid_cols, transcendentals=0
        ),
    )(gt, hid, row_factor[:, :, None], col_factor[:, None, :])
    return update, row_new, col_new.reshape(hid_cols)


def solution(mesh):
    return jax.shard_map(
        body,
        mesh=mesh,
        in_specs=(P("dp", "mp"), P("dp", "mp"), P(None, "dp"), P("mp")),
        out_specs=(P(None, "dp", "mp"), P(None, "dp"), P("mp")),
        check_vma=False,
    )
```

time: 622 us -> 312 us (0.50)
  waiting for transfers between devices: 434 us -> 0 us
  Pallas kernels: 0 us -> 300 us
  matrix products: 58 us -> 0 us
  blocking collectives: 48.7 us -> 0 us
  other arithmetic: 45.2 us -> 1.36 us
  between operations: 14.7 us -> 0.65 us
    pallas_call x0 -> x2, Pallas kernels: none -> 300 us  [the longest x1 237 us: body(): pl.pallas_call(functools.partial(gather_kernel, dp_count, mp_count, piece...]
    all_gather x2 -> x0, waiting for transfers between devices: 278 us -> none  [the longest x1 240 us: body(): lax.all_gather(hidden, 'dp', axis=0, tiled=True)]
    all_to_all x1 -> x0, waiting for transfers between devices: 156 us -> none  [body(): lax.all_to_all(split_out, 'dp', split_axis=2, concat_axis=0, tiled=True)]
    dot_general x1 -> x0, matrix products: 58 us -> none  [body(): lax.dot_general(own_cols, lax.all_gather(hidden, 'dp', axis=0, tiled=True...]
    psum x2 -> x0, blocking collectives: 48.7 us -> none  [the longest x1 37.6 us: body(): scale = lax.psum(jnp.sum(row_new), 'dp') / D]
    convert_element_type x2 -> x0, other arithmetic: 44.6 us -> none  [the longest x1 41.5 us: body(): (grad * lax.rsqrt(row_new[:, None] * col_new[None, :] / scale)).astype(jn...]
    all_to_all x1 -> x0, local copies, waits for them, and re-layouts: 7.56 us -> none  [body(): lax.all_to_all(split_out, 'dp', split_axis=2, concat_axis=0, tiled=True)]
  transfers between devices with their start and end apart: 3 -> 0, of which waited for: 3 -> 0; matrix products, arithmetic and copies ran while one was open for 3% -> 0% of each run, Pallas kernels for 0% -> 0%
where the time goes in v1:
time: 312 us
  Pallas kernels  300 us (96%)
  local copies, waits for them, and re-layouts  9.87 us (3%)
    pallas_call x1, Pallas kernels, body(): pl.pallas_call(functools.partial(gather_kernel, dp_count, mp_count, piece...  237 us
    pallas_call x1, Pallas kernels, body(): pl.pallas_call(update_kernel, grid=(pieces,), out_shape=jax.ShapeDtypeStr...  62.5 us

profile of v1, /device:TPU:0, one launch (start us, length us, event | category | flops | bytes accessed | tf_op | source)
XLA Modules:
  0.0 311.7 jit_solution(11608794033624285280)
XLA Ops:
  0.6 1.4 reshape.16.col_ref
  2.0 2.4 copy.8
  4.4 237.3 %shard_map.67 = (bf16[18,1024,512]{2,1,0:T(8,128)(2,1)}, bf16[4,576,1024]{2,1,0:T(8,128)(2,1)}, f32[4,576]{1,0:T(4,128)}, f32[18,512]{1,0:T(8,128)}, f32[8,128]{1,0:T(8,128)}) custom-call(bf16[128,9216]{1,0:T(8,128)(2,1)} %pre_ref.1, bf16[8,576,128]{2,1,0:T(8,128)(2,1)} %bitcast.6, f32[4,576]{1,0:T(4,128)} %row_ref.1, f32[18,512]{1,0:T(8,128)} %reshape.16.col_ref), custom_call_target="tpu_custom_call" | custom-call | flops 43486543872 | bytes 37748736 | tf_op jit(solution)/shard_map/pallas_call | solution.py:273
  241.7 1.2 slice.3
  242.9 1.4 multiply_bitcast_fusion
  244.3 1.4 reshape.17
  245.7 0.8 rsqrt.7
  246.5 0.6 broadcast_in_dim.7.col_ref
  247.2 1.4 copy.9.row_ref
  248.6 0.0 copy-start
  248.6 62.5 %shard_map.68 = bf16[4,576,9216]{2,1,0:T(8,128)(2,1)} custom-call(bf16[4,576,1024]{2,1,0:T(8,128)(2,1)} %get-tuple-element.8.gt_ref, bf16[18,1024,512]{2,1,0:T(8,128)(2,1)} %get-tuple-element.9.hid_ref, f32[4,576,1]{2,1,0:T(8,128)} %copy.9.row_ref, f32[18,1,512]{2,1,0:T(1,128)} %broadcast_in_dim.7.col_ref), custom_call_target="tpu_custom_call" | custom-call | flops 43486543872 | bytes 61341696 | tf_op jit(solution)/shard_map/pallas_call | solution.py:305
  311.1 0.0 copy-done
  311.1 0.6 copy.11
Async XLA Ops:
  248.6 62.5 %copy-start = (f32[4,576]{1,0:T(4,128)S(1)}, f32[4,576]{1,0:T(4,128)}, u32[]{:S(2)}) copy-start(f32[4,576]{1,0:T(4,128)} %get-tuple-element.17) | copy-start | bytes 27652

commit v2 on v1

--- a/solution.py
+++ b/solution.py
@@ -14,19 +14,20 @@
 decay = 1.0 - 2.0 ** (-0.8)
 tiny = 1e-30
 
-PIECES = 18
-G_SEND_STEP = 2
-G_READY_STEP = 8
+MIN_PIECES = 18
+SKEW = 2
+G_SEND_STEP = 4
+G_READY_STEP = 16
 
 
 def gather_kernel(
     dp_count, mp_count, pieces,
     pre_ref, g_ref, row_ref, col_ref,
-    hid_out, gt_out, row_new, col_new, scale_out,
-    hid, gt, row_acc, row_part, col_part, total_part,
+    hid_out, gt_out, kept_out, row_new, col_new, scale_out,
+    hid, gt, kept, row_acc, row_part, col_part, total_part,
     up_sem, down_sem, side_sem, recv_sem,
     g_local, g_send, g_recv, m_send, m_recv,
-    out_sem, gt_sem, r_send, r_recv, c_send, c_recv, t_send, t_recv,
+    out_sem, kept_sem, gt_sem, r_send, r_recv, c_send, c_recv, t_send, t_recv,
 ):
     rows = pre_ref.shape[0]
     width = hid.shape[2]
@@ -127,13 +128,13 @@
                 push(go, src, p, up, down, side)
 
         for k in range(1, depth):
-            p = t - k
+            p = t - SKEW * k
             live = (p >= 0) & (p < pieces)
             row_first = jnp.logical_not(side_first(p))
             passing(z - k, y, p, live & (z - k >= 0), up_ok, None, row_first)
             passing(z + k, y, p, live & (z + k < depth), None, down_ok, row_first)
         for k in range(depth):
-            p = t - k - 1
+            p = t - SKEW * (k + 1)
             live = (p >= 0) & (p < pieces) & side_first(p)
             if k == 0:
                 passing(z, 1 - y, p, live, up_ok, down_ok, None)
@@ -143,17 +144,33 @@
 
     row_acc[...] = jnp.zeros_like(row_acc)
 
+    def keep(half):
+        slot = lax.rem(half, 2)
+        return pltpu.make_async_copy(kept.at[slot], kept_out.at[half], kept_sem.at[slot])
+
     def work(c):
         @pl.when(jnp.logical_not(side_first(c)))
         def _():
             for zs in range(depth):
                 arrive(zs * 2 + 1 - y, c)
 
-        pltpu.make_async_copy(hid.at[c], hid_out.at[c], out_sem.at[c]).start()
+        half = c // 2
+        even = lax.rem(c, 2) == 0
+        slot = jnp.where(even, lax.rem(half, 2), 2)
+
+        @pl.when(jnp.logical_not(even))
+        def _():
+            pltpu.make_async_copy(hid.at[c], hid_out.at[half], out_sem.at[half]).start()
+
+        @pl.when(even & (half >= 2))
+        def _():
+            keep(half - 2).wait()
+
         block = hid[c]
 
         def one(m, col):
             prod = jnp.dot(gt[m], block, preferred_element_type=jnp.float32)
+            kept[slot, m] = prod
             sq = prod * prod
             part = sq[:, 0:128]
             for q in range(1, width // 128):
@@ -164,10 +181,14 @@
         col = lax.fori_loop(0, mp_count, one, jnp.zeros((1, width), jnp.float32))
         col_part[d, pl.ds(c, 1), :] = col
 
+        @pl.when(even)
+        def _():
+            keep(half).start()
+
     def done_by(t):
-        return jnp.clip(jnp.minimum(2 * (t - G_READY_STEP + 1), t - depth + 1), 0, pieces)
-
-    steps = pieces + depth
+        return jnp.clip(jnp.minimum(2 * (t - G_READY_STEP + 1), t - SKEW * depth + 1), 0, pieces)
+
+    steps = pieces + SKEW * depth
 
     @pl.loop(0, steps)
     def _(t):
@@ -241,19 +262,34 @@
         remote(row_part.at[a], row_part.at[a], r_send.at[j], r_recv.at[j], (d, mate(j))).wait_send()
     pltpu.make_async_copy(gt, gt_out, gt_sem).wait()
 
-    @pl.loop(0, pieces)
+    keep(pieces // 2 - 2).wait()
+    keep(pieces // 2 - 1).wait()
+
+    @pl.loop(0, pieces // 2)
     def _(c):
-        pltpu.make_async_copy(hid.at[c], hid_out.at[c], out_sem.at[c]).wait()
-
-
-def update_kernel(gt_ref, hid_ref, row_ref, col_ref, out_ref):
+        pltpu.make_async_copy(hid.at[2 * c + 1], hid_out.at[c], out_sem.at[c]).wait()
+
+
+def update_kernel(tokens, gt_ref, hid_ref, kept_ref, row_ref, col_ref, scale_ref, out_ref, factor):
+    i = pl.program_id(0)
+    width = hid_ref.shape[2]
+
+    @pl.when(i == 0)
+    def _():
+        row = lax.rsqrt(row_ref[...] / scale_ref[0:1, 0:1]) / tokens
+        for m in range(row_ref.shape[0]):
+            factor[m] = jnp.broadcast_to(row[m:m + 1], (128, row.shape[1])).T
+
     block = hid_ref[0]
-    col = col_ref[0]
+    left = lax.rsqrt(col_ref[pl.ds(2 * i, 1), :])
+    right = lax.rsqrt(col_ref[pl.ds(2 * i + 1, 1), :])
 
     @pl.loop(0, gt_ref.shape[0])
     def _(m):
+        row = jnp.concatenate([factor[m]] * (width // 128), axis=1)
         prod = jnp.dot(gt_ref[m], block, preferred_element_type=jnp.float32)
-        out_ref[m] = (prod * row_ref[m] * col).astype(jnp.bfloat16)
+        out_ref[m, :, 0:width] = (kept_ref[0, m] * row * left).astype(jnp.bfloat16)
+        out_ref[m, :, width:2 * width] = (prod * row * right).astype(jnp.bfloat16)
 
 
 def body(pre_act, grad_out, row_state, col_state):
@@ -262,35 +298,37 @@
     rows, hid_cols = pre_act.shape
     tokens = rows * dp_count
     slice_width = row_state.shape[1]
-    pieces = PIECES
-    width = hid_cols // pieces
+    width = 256 if hid_cols % 512 == 0 and hid_cols // 256 >= MIN_PIECES else 128
+    pieces = hid_cols // width
     f32, bf16 = jnp.float32, jnp.bfloat16
     g_blocks = grad_out.reshape(rows, dp_count, slice_width).transpose(1, 2, 0)
     whole = pl.BlockSpec(memory_space=VMEM)
     anywhere = pl.BlockSpec(memory_space=pl.ANY)
     dma = pltpu.SemaphoreType.DMA
     flops = 2 * tokens * mp_count * slice_width * hid_cols
-    hid, gt, row_new, col_new, scale = pl.pallas_call(
+    hid, gt, kept, row_new, col_new, scale = pl.pallas_call(
         functools.partial(gather_kernel, dp_count, mp_count, pieces),
         out_shape=(
-            jax.ShapeDtypeStruct((pieces, tokens, width), bf16),
+            jax.ShapeDtypeStruct((pieces // 2, tokens, width), bf16),
             jax.ShapeDtypeStruct((mp_count, slice_width, tokens), bf16),
+            jax.ShapeDtypeStruct((pieces // 2, mp_count, slice_width, width), f32),
             jax.ShapeDtypeStruct((mp_count, slice_width), f32),
             jax.ShapeDtypeStruct((pieces, width), f32),
             jax.ShapeDtypeStruct((8, 128), f32),
         ),
         in_specs=[whole] * 4,
-        out_specs=(anywhere, anywhere, whole, whole, whole),
+        out_specs=(anywhere, anywhere, anywhere, whole, whole, whole),
         scratch_shapes=[
             VMEM((pieces, tokens, width), bf16),
             VMEM((mp_count, slice_width, tokens), bf16),
+            VMEM((3, mp_count, slice_width, width), f32),
             VMEM((mp_count, slice_width, 128), f32),
             VMEM((mp_count, mp_count, slice_width), f32),
             VMEM((dp_count, pieces, width), f32),
             VMEM((dp_count, 8, 128), f32),
             dma((dp_count, pieces)), dma((dp_count, pieces)), dma((dp_count, pieces)), dma((dp_count, pieces)),
             dma, dma((dp_count,)), dma((dp_count,)), dma((mp_count,)), dma((mp_count,)),
-            dma((pieces,)), dma, dma((mp_count,)), dma((mp_count,)),
+            dma((pieces // 2,)), dma((2,)), dma, dma((mp_count,)), dma((mp_count,)),
             dma((dp_count,)), dma((dp_count,)), dma((dp_count,)), dma((dp_count,)),
         ],
         compiler_params=pltpu.CompilerParams(
@@ -300,24 +338,25 @@
             flops=flops, bytes_accessed=2 * tokens * hid_cols * 2, transcendentals=rows * hid_cols
         ),
     )(pre_act, g_blocks, row_state, col_state.reshape(pieces, width))
-    row_factor = lax.rsqrt(row_new / scale[0, 0]) / tokens
-    col_factor = lax.rsqrt(col_new)
     update = pl.pallas_call(
-        update_kernel,
-        grid=(pieces,),
+        functools.partial(update_kernel, tokens),
+        grid=(pieces // 2,),
         out_shape=jax.ShapeDtypeStruct((mp_count, slice_width, hid_cols), bf16),
         in_specs=[
             pl.BlockSpec((mp_count, slice_width, tokens), lambda i: (0, 0, 0)),
             pl.BlockSpec((1, tokens, width), lambda i: (i, 0, 0)),
-            pl.BlockSpec((mp_count, slice_width, 1), lambda i: (0, 0, 0)),
-            pl.BlockSpec((1, 1, width), lambda i: (i, 0, 0)),
+            pl.BlockSpec((1, mp_count, slice_width, width), lambda i: (i, 0, 0, 0)),
+            pl.BlockSpec((mp_count, slice_width), lambda i: (0, 0)),
+            pl.BlockSpec((pieces, width), lambda i: (0, 0)),
+            pl.BlockSpec((8, 128), lambda i: (0, 0)),
         ],
-        out_specs=pl.BlockSpec((mp_count, slice_width, width), lambda i: (0, 0, i)),
+        out_specs=pl.BlockSpec((mp_count, slice_width, 2 * width), lambda i: (0, 0, i)),
+        scratch_shapes=[VMEM((mp_count, slice_width, 128), f32)],
         compiler_params=pltpu.CompilerParams(vmem_limit_bytes=56 * 2**20),
         cost_estimate=pl.CostEstimate(
-            flops=flops, bytes_accessed=2 * (tokens + mp_count * slice_width) * hid_cols, transcendentals=0
+            flops=flops // 2, bytes_accessed=(tokens + 4 * mp_count * slice_width) * hid_cols, transcendentals=0
         ),
-    )(gt, hid, row_factor[:, :, None], col_factor[:, None, :])
+    )(gt, hid, kept, row_new, col_new, scale)
     return update, row_new, col_new.reshape(hid_cols)
 
 

time: 312 us -> 297 us (0.952)
  Pallas kernels: 300 us -> 290 us
  local copies, waits for them, and re-layouts: 9.87 us -> 4.98 us
    pallas_call x1, Pallas kernels: 62.5 us -> 47.9 us  [body(): pl.pallas_call(functools.partial(update_kernel, tokens), grid=(pieces //...]
    pallas_call x1, Pallas kernels: 237 us -> 243 us  [body(): pl.pallas_call(functools.partial(gather_kernel, dp_count, mp_count, piece...]
where the time goes in v2:
time: 297 us; the launch traced here: 296 us
  Pallas kernels  290 us (98%)
  local copies, waits for them, and re-layouts  4.98 us (2%)
    pallas_call x1, Pallas kernels, body(): pl.pallas_call(functools.partial(gather_kernel, dp_count, mp_count, piece...  243 us
    pallas_call x1, Pallas kernels, body(): pl.pallas_call(functools.partial(update_kernel, tokens), grid=(pieces //...  47.9 us

profile of v2, /device:TPU:0, one launch (start us, length us, event | category | flops | bytes accessed | tf_op | source)
XLA Modules:
  0.0 296.1 jit_solution(2089560047589816790)
XLA Ops:
  0.6 1.4 reshape.16.col_ref
  2.0 2.4 copy.7
  4.4 242.6 %shard_map.67 = (bf16[18,1024,256]{2,1,0:T(8,128)(2,1)}, bf16[4,576,1024]{2,1,0:T(8,128)(2,1)}, f32[18,4,576,256]{3,2,1,0:T(8,128)}, f32[4,576]{1,0:T(4,128)}, f32[36,256]{1,0:T(8,128)}, /*index=5*/f32[8,128]{1,0:T(8,128)}) custom-call(bf16[128,9216]{1,0:T(8,128)(2,1)} %pre_ref.1, bf16[8,576,128]{2,1,0:T(8,128)(2,1)} %bitcast.3, f32[4,576]{1,0:T(4,128)} %row_ref.1, ...), custom_call_target="tpu_custom_call" | custom-call | flops 43486543872 | bytes 37748736 | tf_op jit(solution)/shard_map/pallas_call | solution.py:309
  247.0 0.0 copy-start
  247.0 0.0 copy-start.1
  247.0 47.9 %shard_map.68 = bf16[4,576,9216]{2,1,0:T(8,128)(2,1)} custom-call(bf16[4,576,1024]{2,1,0:T(8,128)(2,1)} %get-tuple-element.9.gt_ref, bf16[18,1024,256]{2,1,0:T(8,128)(2,1)} %get-tuple-element.10.hid_ref, f32[18,4,576,256]{3,2,1,0:T(8,128)} %get-tuple-element.11.kept_ref, f32[4,576]{1,0:T(4,128)} %get-tuple-element.19.row_ref, ...), custom_call_target="tpu_custom_call" | custom-call | flops 21743271936 | bytes 94371840 | tf_op jit(solution)/shard_map/pallas_call | solution.py:341
  294.9 0.0 copy-done
  294.9 0.6 reshape.17
  295.5 0.0 copy-done.1
  295.5 0.6 copy.9
Async XLA Ops:
  247.0 47.9 %copy-start = (f32[36,256]{1,0:T(8,128)S(1)}, f32[36,256]{1,0:T(8,128)}, u32[]{:S(2)}) copy-start(f32[36,256]{1,0:T(8,128)} %get-tuple-element.13.col_ref) | copy-start | bytes 110596
  247.0 48.5 %copy-start.1 = (f32[4,576]{1,0:T(4,128)S(1)}, f32[4,576]{1,0:T(4,128)}, u32[]{:S(2)}) copy-start(f32[4,576]{1,0:T(4,128)} %get-tuple-element.19.row_ref) | copy-start | bytes 27652

commit v3 on v2

--- a/solution.py
+++ b/solution.py
@@ -16,6 +16,7 @@
 
 MIN_PIECES = 18
 SKEW = 2
+DRAIN_LAG = 6
 G_SEND_STEP = 4
 G_READY_STEP = 16
 
@@ -38,7 +39,7 @@
     a = lax.axis_index("mp")
     z = d // 2
     y = d % 2
-    period = 2 * max(depth - 1, 1)
+    period = 2 * max(depth, 1)
 
     def peer(i):
         return lax.rem(d + i, dp_count)
@@ -90,7 +91,7 @@
         remote(block, block, side_sem.at[src, p], recv_sem.at[src, p], (d, a)).wait_recv()
 
     def side_first(p):
-        return lax.rem(p, period) == min(2, period - 1)
+        return lax.rem(p, period) == min(4, period - 1)
 
     def push(go, src, p, up, down, side):
         block = block_of(src, p)
@@ -194,6 +195,10 @@
     def _(t):
         events(t, True)
 
+        @pl.when(t >= DRAIN_LAG)
+        def _():
+            events(t - DRAIN_LAG, False)
+
         @pl.when(t == G_SEND_STEP)
         def _():
             spread_g()
@@ -217,6 +222,10 @@
         remote(row_part.at[a], row_part.at[a], r_send.at[j], r_recv.at[j], (d, mate(j))).start()
     for i in range(1, dp_count):
         remote(col_part.at[d], col_part.at[d], c_send.at[i], c_recv.at[i], (peer(i), a)).start()
+
+    @pl.loop(steps - DRAIN_LAG, steps)
+    def _(t):
+        events(t, False)
 
     for j in range(1, mp_count):
         src = lax.rem(a - j + mp_count, mp_count)
@@ -249,10 +258,6 @@
         total = total + total_part[i]
     scale_out[...] = total / D
 
-    @pl.loop(0, steps)
-    def _(t):
-        events(t, False)
-
     for i in range(1, dp_count):
         remote(g_ref.at[peer(i)], gt.at[a, :, tok(d)], g_send.at[i], g_recv.at[i], (peer(i), a)).wait_send()
         remote(col_part.at[d], col_part.at[d], c_send.at[i], c_recv.at[i], (peer(i), a)).wait_send()
@@ -284,12 +289,13 @@
     left = lax.rsqrt(col_ref[pl.ds(2 * i, 1), :])
     right = lax.rsqrt(col_ref[pl.ds(2 * i + 1, 1), :])
 
-    @pl.loop(0, gt_ref.shape[0])
-    def _(m):
+    prod = jnp.dot(gt_ref[...], block, preferred_element_type=jnp.float32)
+    count, slice_width = row_ref.shape
+    for m in range(count):
         row = jnp.concatenate([factor[m]] * (width // 128), axis=1)
-        prod = jnp.dot(gt_ref[m], block, preferred_element_type=jnp.float32)
+        part = prod[m * slice_width:(m + 1) * slice_width]
         out_ref[m, :, 0:width] = (kept_ref[0, m] * row * left).astype(jnp.bfloat16)
-        out_ref[m, :, width:2 * width] = (prod * row * right).astype(jnp.bfloat16)
+        out_ref[m, :, width:2 * width] = (part * row * right).astype(jnp.bfloat16)
 
 
 def body(pre_act, grad_out, row_state, col_state):
@@ -343,7 +349,7 @@
         grid=(pieces // 2,),
         out_shape=jax.ShapeDtypeStruct((mp_count, slice_width, hid_cols), bf16),
         in_specs=[
-            pl.BlockSpec((mp_count, slice_width, tokens), lambda i: (0, 0, 0)),
+            pl.BlockSpec((mp_count * slice_width, tokens), lambda i: (0, 0)),
             pl.BlockSpec((1, tokens, width), lambda i: (i, 0, 0)),
             pl.BlockSpec((1, mp_count, slice_width, width), lambda i: (i, 0, 0, 0)),
             pl.BlockSpec((mp_count, slice_width), lambda i: (0, 0)),
@@ -356,7 +362,7 @@
         cost_estimate=pl.CostEstimate(
             flops=flops // 2, bytes_accessed=(tokens + 4 * mp_count * slice_width) * hid_cols, transcendentals=0
         ),
-    )(gt, hid, kept, row_new, col_new, scale)
+    )(gt.reshape(mp_count * slice_width, tokens), hid, kept, row_new, col_new, scale)
     return update, row_new, col_new.reshape(hid_cols)
 
 

time: 297 us -> 295 us (level)
  no operation moved by 1% of the time
where the time goes in v3:
time: 295 us
  Pallas kernels  289 us (98%)
  local copies, waits for them, and re-layouts  4.98 us (2%)
    pallas_call x1, Pallas kernels, body(): pl.pallas_call(functools.partial(gather_kernel, dp_count, mp_count, piece...  242 us
    pallas_call x1, Pallas kernels, body(): pl.pallas_call(functools.partial(update_kernel, tokens), grid=(pieces //...  46.7 us

profile of v3, /device:TPU:0, one launch (start us, length us, event | category | flops | bytes accessed | tf_op | source)
XLA Modules:
  0.0 294.6 jit_solution(7550151318345882079)
XLA Ops:
  0.6 1.4 reshape.19.col_ref
  2.0 2.4 copy.7
  4.4 242.2 %shard_map.67 = (bf16[18,1024,256]{2,1,0:T(8,128)(2,1)}, bf16[4,576,1024]{2,1,0:T(8,128)(2,1)}, f32[18,4,576,256]{3,2,1,0:T(8,128)}, f32[4,576]{1,0:T(4,128)}, f32[36,256]{1,0:T(8,128)}, /*index=5*/f32[8,128]{1,0:T(8,128)}) custom-call(bf16[128,9216]{1,0:T(8,128)(2,1)} %pre_ref.1, bf16[8,576,128]{2,1,0:T(8,128)(2,1)} %bitcast.5, f32[4,576]{1,0:T(4,128)} %row_ref.1, ...), custom_call_target="tpu_custom_call" | custom-call | flops 43486543872 | bytes 37748736 | tf_op jit(solution)/shard_map/pallas_call | solution.py:315
  246.6 0.0 copy-start
  246.7 0.0 copy-start.1
  246.7 46.7 %shard_map.68 = bf16[4,576,9216]{2,1,0:T(8,128)(2,1)} custom-call(bf16[2304,1024]{1,0:T(8,128)(2,1)} %bitcast.4, bf16[18,1024,256]{2,1,0:T(8,128)(2,1)} %get-tuple-element.10.hid_ref, f32[18,4,576,256]{3,2,1,0:T(8,128)} %get-tuple-element.11.kept_ref, f32[4,576]{1,0:T(4,128)} %get-tuple-element.19.row_ref, f32[36,256]{1,0:T(8,128)} %get-tuple-element.13.col_ref, ...), custom_call_target="tpu_custom_call" | custom-call | flops 21743271936 | bytes 94371840 | tf_op jit(solution)/shard_map/pallas_call | solution.py:347
  293.4 0.0 copy-done
  293.4 0.6 reshape.21
  294.0 0.0 copy-done.1
  294.0 0.6 copy.9
Async XLA Ops:
  246.6 46.7 %copy-start = (f32[36,256]{1,0:T(8,128)S(1)}, f32[36,256]{1,0:T(8,128)}, u32[]{:S(2)}) copy-start(f32[36,256]{1,0:T(8,128)} %get-tuple-element.13.col_ref) | copy-start | bytes 110596
  246.7 47.3 %copy-start.1 = (f32[4,576]{1,0:T(4,128)S(1)}, f32[4,576]{1,0:T(4,128)}, u32[]{:S(2)}) copy-start(f32[4,576]{1,0:T(4,128)} %get-tuple-element.19.row_ref) | copy-start | bytes 27652

commit v4 on v3

--- a/solution.py
+++ b/solution.py
@@ -18,17 +18,18 @@
 SKEW = 2
 DRAIN_LAG = 6
 G_SEND_STEP = 4
-G_READY_STEP = 16
+G_PASS_STEP = 10
+G_READY_STEP = 11
 
 
 def gather_kernel(
     dp_count, mp_count, pieces,
     pre_ref, g_ref, row_ref, col_ref,
-    hid_out, gt_out, kept_out, row_new, col_new, scale_out,
+    kept_out, row_new, col_new, scale_out,
     hid, gt, kept, row_acc, row_part, col_part, total_part,
     up_sem, down_sem, side_sem, recv_sem,
-    g_local, g_send, g_recv, m_send, m_recv,
-    out_sem, kept_sem, gt_sem, r_send, r_recv, c_send, c_recv, t_send, t_recv,
+    g_local, g_send, g_recv, m_send, m_recv, n_send,
+    kept_sem, r_send, r_recv, c_send, c_recv, t_send, t_recv,
 ):
     rows = pre_ref.shape[0]
     width = hid.shape[2]
@@ -75,13 +76,40 @@
             block = gt.at[a, :, tok(src)]
             remote(block, block, g_send.at[i], g_recv.at[i], (peer(i), a)).wait_recv()
         for j in range(1, mp_count):
-            remote(gt.at[a], gt.at[a], m_send.at[j], m_recv.at[j], (d, mate(j))).start()
+            send_g(j, True)
+
+    def twin_of(m):
+        return m + 1 - 2 * lax.rem(m, 2)
+
+    twin = twin_of(a)
+
+    def slab(m, send, dev):
+        return remote(gt.at[m], gt.at[m], send, m_recv.at[m], (d, dev))
+
+    def send_g(j, go):
+        dst = mate(j)
+
+        def act():
+            copy = slab(a, m_send.at[j], dst)
+            if go:
+                copy.start()
+            else:
+                copy.wait_send()
+
+        if j % 2 == 0:
+            act()
+        else:
+            pl.when(dst == twin)(act)
+
+    def pass_g():
+        for j in range(2, mp_count, 2):
+            src = mate(j)
+            slab(src, n_send.at[j], twin).wait_recv()
+            slab(src, n_send.at[j], twin).start()
 
     def finish_g():
-        for j in range(1, mp_count):
-            src = lax.rem(a - j + mp_count, mp_count)
-            remote(gt.at[src], gt.at[src], m_send.at[j], m_recv.at[j], (d, mate(j))).wait_recv()
-        pltpu.make_async_copy(gt, gt_out, gt_sem).start()
+        for j in range(1, mp_count, 2):
+            slab(mate(j), n_send.at[j], twin).wait_recv()
 
     def block_of(src, p):
         return hid.at[p, tok(src)]
@@ -145,9 +173,9 @@
 
     row_acc[...] = jnp.zeros_like(row_acc)
 
-    def keep(half):
-        slot = lax.rem(half, 2)
-        return pltpu.make_async_copy(kept.at[slot], kept_out.at[half], kept_sem.at[slot])
+    def keep(c):
+        slot = lax.rem(c, 2)
+        return pltpu.make_async_copy(kept.at[slot], kept_out.at[c], kept_sem.at[slot])
 
     def work(c):
         @pl.when(jnp.logical_not(side_first(c)))
@@ -155,21 +183,16 @@
             for zs in range(depth):
                 arrive(zs * 2 + 1 - y, c)
 
-        half = c // 2
-        even = lax.rem(c, 2) == 0
-        slot = jnp.where(even, lax.rem(half, 2), 2)
-
-        @pl.when(jnp.logical_not(even))
-        def _():
-            pltpu.make_async_copy(hid.at[c], hid_out.at[half], out_sem.at[half]).start()
-
-        @pl.when(even & (half >= 2))
-        def _():
-            keep(half - 2).wait()
+        slot = lax.rem(c, 2)
+
+        @pl.when(c >= 2)
+        def _():
+            keep(c - 2).wait()
 
         block = hid[c]
 
-        def one(m, col):
+        col = jnp.zeros((1, width), jnp.float32)
+        for m in range(mp_count):
             prod = jnp.dot(gt[m], block, preferred_element_type=jnp.float32)
             kept[slot, m] = prod
             sq = prod * prod
@@ -177,14 +200,9 @@
             for q in range(1, width // 128):
                 part = part + sq[:, q * 128:(q + 1) * 128]
             row_acc[m] += part
-            return col + jnp.sum(sq, axis=0, keepdims=True)
-
-        col = lax.fori_loop(0, mp_count, one, jnp.zeros((1, width), jnp.float32))
+            col = col + jnp.sum(sq, axis=0, keepdims=True)
         col_part[d, pl.ds(c, 1), :] = col
-
-        @pl.when(even)
-        def _():
-            keep(half).start()
+        keep(c).start()
 
     def done_by(t):
         return jnp.clip(jnp.minimum(2 * (t - G_READY_STEP + 1), t - SKEW * depth + 1), 0, pieces)
@@ -202,6 +220,10 @@
         @pl.when(t == G_SEND_STEP)
         def _():
             spread_g()
+
+        @pl.when(t == G_PASS_STEP)
+        def _():
+            pass_g()
 
         @pl.when(t == G_READY_STEP)
         def _():
@@ -263,21 +285,17 @@
         remote(col_part.at[d], col_part.at[d], c_send.at[i], c_recv.at[i], (peer(i), a)).wait_send()
         remote(total_part.at[d], total_part.at[d], t_send.at[i], t_recv.at[i], (peer(i), a)).wait_send()
     for j in range(1, mp_count):
-        remote(gt.at[a], gt.at[a], m_send.at[j], m_recv.at[j], (d, mate(j))).wait_send()
+        send_g(j, False)
+        if j % 2 == 0:
+            slab(mate(j), n_send.at[j], twin).wait_send()
         remote(row_part.at[a], row_part.at[a], r_send.at[j], r_recv.at[j], (d, mate(j))).wait_send()
-    pltpu.make_async_copy(gt, gt_out, gt_sem).wait()
-
-    keep(pieces // 2 - 2).wait()
-    keep(pieces // 2 - 1).wait()
-
-    @pl.loop(0, pieces // 2)
-    def _(c):
-        pltpu.make_async_copy(hid.at[2 * c + 1], hid_out.at[c], out_sem.at[c]).wait()
-
-
-def update_kernel(tokens, gt_ref, hid_ref, kept_ref, row_ref, col_ref, scale_ref, out_ref, factor):
+    keep(pieces - 2).wait()
+    keep(pieces - 1).wait()
+
+
+def update_kernel(tokens, kept_ref, row_ref, col_ref, scale_ref, out_ref, factor):
     i = pl.program_id(0)
-    width = hid_ref.shape[2]
+    count, width = kept_ref.shape[0], kept_ref.shape[3]
 
     @pl.when(i == 0)
     def _():
@@ -285,17 +303,13 @@
         for m in range(row_ref.shape[0]):
             factor[m] = jnp.broadcast_to(row[m:m + 1], (128, row.shape[1])).T
 
-    block = hid_ref[0]
-    left = lax.rsqrt(col_ref[pl.ds(2 * i, 1), :])
-    right = lax.rsqrt(col_ref[pl.ds(2 * i + 1, 1), :])
-
-    prod = jnp.dot(gt_ref[...], block, preferred_element_type=jnp.float32)
-    count, slice_width = row_ref.shape
-    for m in range(count):
+    cols = [lax.rsqrt(col_ref[pl.ds(count * i + n, 1), :]) for n in range(count)]
+
+    @pl.loop(0, row_ref.shape[0])
+    def _(m):
         row = jnp.concatenate([factor[m]] * (width // 128), axis=1)
-        part = prod[m * slice_width:(m + 1) * slice_width]
-        out_ref[m, :, 0:width] = (kept_ref[0, m] * row * left).astype(jnp.bfloat16)
-        out_ref[m, :, width:2 * width] = (part * row * right).astype(jnp.bfloat16)
+        for n in range(count):
+            out_ref[m, :, n * width:(n + 1) * width] = (kept_ref[n, m] * row * cols[n]).astype(jnp.bfloat16)
 
 
 def body(pre_act, grad_out, row_state, col_state):
@@ -312,29 +326,27 @@
     anywhere = pl.BlockSpec(memory_space=pl.ANY)
     dma = pltpu.SemaphoreType.DMA
     flops = 2 * tokens * mp_count * slice_width * hid_cols
-    hid, gt, kept, row_new, col_new, scale = pl.pallas_call(
+    kept, row_new, col_new, scale = pl.pallas_call(
         functools.partial(gather_kernel, dp_count, mp_count, pieces),
         out_shape=(
-            jax.ShapeDtypeStruct((pieces // 2, tokens, width), bf16),
-            jax.ShapeDtypeStruct((mp_count, slice_width, tokens), bf16),
-            jax.ShapeDtypeStruct((pieces // 2, mp_count, slice_width, width), f32),
+            jax.ShapeDtypeStruct((pieces, mp_count, slice_width, width), f32),
             jax.ShapeDtypeStruct((mp_count, slice_width), f32),
             jax.ShapeDtypeStruct((pieces, width), f32),
             jax.ShapeDtypeStruct((8, 128), f32),
         ),
         in_specs=[whole] * 4,
-        out_specs=(anywhere, anywhere, anywhere, whole, whole, whole),
+        out_specs=(anywhere, whole, whole, whole),
         scratch_shapes=[
             VMEM((pieces, tokens, width), bf16),
             VMEM((mp_count, slice_width, tokens), bf16),
-            VMEM((3, mp_count, slice_width, width), f32),
+            VMEM((2, mp_count, slice_width, width), f32),
             VMEM((mp_count, slice_width, 128), f32),
             VMEM((mp_count, mp_count, slice_width), f32),
             VMEM((dp_count, pieces, width), f32),
             VMEM((dp_count, 8, 128), f32),
             dma((dp_count, pieces)), dma((dp_count, pieces)), dma((dp_count, pieces)), dma((dp_count, pieces)),
-            dma, dma((dp_count,)), dma((dp_count,)), dma((mp_count,)), dma((mp_count,)),
-            dma((pieces // 2,)), dma((2,)), dma, dma((mp_count,)), dma((mp_count,)),
+            dma, dma((dp_count,)), dma((dp_count,)), dma((mp_count,)), dma((mp_count,)), dma((mp_count,)),
+            dma((2,)), dma((mp_count,)), dma((mp_count,)),
             dma((dp_count,)), dma((dp_count,)), dma((dp_count,)), dma((dp_count,)),
         ],
         compiler_params=pltpu.CompilerParams(
@@ -349,9 +361,7 @@
         grid=(pieces // 2,),
         out_shape=jax.ShapeDtypeStruct((mp_count, slice_width, hid_cols), bf16),
         in_specs=[
-            pl.BlockSpec((mp_count * slice_width, tokens), lambda i: (0, 0)),
-            pl.BlockSpec((1, tokens, width), lambda i: (i, 0, 0)),
-            pl.BlockSpec((1, mp_count, slice_width, width), lambda i: (i, 0, 0, 0)),
+            pl.BlockSpec((2, mp_count, slice_width, width), lambda i: (i, 0, 0, 0)),
             pl.BlockSpec((mp_count, slice_width), lambda i: (0, 0)),
             pl.BlockSpec((pieces, width), lambda i: (0, 0)),
             pl.BlockSpec((8, 128), lambda i: (0, 0)),
@@ -360,9 +370,9 @@
         scratch_shapes=[VMEM((mp_count, slice_width, 128), f32)],
         compiler_params=pltpu.CompilerParams(vmem_limit_bytes=56 * 2**20),
         cost_estimate=pl.CostEstimate(
-            flops=flops // 2, bytes_accessed=(tokens + 4 * mp_count * slice_width) * hid_cols, transcendentals=0
+            flops=2 * mp_count * slice_width * hid_cols, bytes_accessed=6 * mp_count * slice_width * hid_cols, transcendentals=0
         ),
-    )(gt.reshape(mp_count * slice_width, tokens), hid, kept, row_new, col_new, scale)
+    )(kept, row_new, col_new, scale)
     return update, row_new, col_new.reshape(hid_cols)
 
 

time: 295 us -> 290 us (0.983)
  Pallas kernels: 289 us -> 284 us
where the time goes in v4:
time: 290 us
  Pallas kernels  284 us (98%)
  local copies, waits for them, and re-layouts  4.99 us (2%)
    pallas_call x1, Pallas kernels, body(): pl.pallas_call(functools.partial(gather_kernel, dp_count, mp_count, piece...  240 us
    pallas_call x1, Pallas kernels, body(): pl.pallas_call(functools.partial(update_kernel, tokens), grid=(pieces //...  43.9 us

profile of v4, /device:TPU:0, one launch (start us, length us, event | category | flops | bytes accessed | tf_op | source)
XLA Modules:
  0.0 289.8 jit_solution(11925097205320898289)
XLA Ops:
  0.6 1.4 reshape.16.col_ref
  2.0 2.4 copy.7
  4.4 240.3 %shard_map.67 = (f32[36,4,576,256]{3,2,1,0:T(8,128)}, f32[4,576]{1,0:T(4,128)}, f32[36,256]{1,0:T(8,128)}, f32[8,128]{1,0:T(8,128)}) custom-call(bf16[128,9216]{1,0:T(8,128)(2,1)} %pre_ref.1, bf16[8,576,128]{2,1,0:T(8,128)(2,1)} %bitcast.3, f32[4,576]{1,0:T(4,128)} %row_ref.1, f32[36,256]{1,0:T(8,128)} %reshape.16.col_ref), custom_call_target="tpu_custom_call" | custom-call | flops 43486543872 | bytes 37748736 | tf_op jit(solution)/shard_map/pallas_call | solution.py:329
  244.7 0.0 copy-start
  244.8 0.0 copy-start.1
  244.8 43.9 %shard_map.68 = bf16[4,576,9216]{2,1,0:T(8,128)(2,1)} custom-call(f32[36,4,576,256]{3,2,1,0:T(8,128)} %get-tuple-element.7.kept_ref, f32[4,576]{1,0:T(4,128)} %get-tuple-element.15.row_ref, f32[36,256]{1,0:T(8,128)} %get-tuple-element.9.col_ref, f32[8,128]{1,0:T(8,128)} %get-tuple-element.10.scale_ref), custom_call_target="tpu_custom_call" | custom-call | flops 42467328 | bytes 127401984 | tf_op jit(solution)/shard_map/pallas_call | solution.py:359
  288.6 0.0 copy-done
  288.6 0.6 reshape.17
  289.2 0.0 copy-done.1
  289.2 0.6 copy.9
Async XLA Ops:
  244.7 43.9 %copy-start = (f32[36,256]{1,0:T(8,128)S(1)}, f32[36,256]{1,0:T(8,128)}, u32[]{:S(2)}) copy-start(f32[36,256]{1,0:T(8,128)} %get-tuple-element.9.col_ref) | copy-start | bytes 110596
  244.8 44.5 %copy-start.1 = (f32[4,576]{1,0:T(4,128)S(1)}, f32[4,576]{1,0:T(4,128)}, u32[]{:S(2)}) copy-start(f32[4,576]{1,0:T(4,128)} %get-tuple-element.15.row_ref) | copy-start | bytes 27652
